TPU v7x, 256 devices: a whole 4x4x8 slice. The times are simulated.
256 devices in a mesh: group: 16 (over y, x), ingroup: 16 (over z, core).
Axes of the slice: x: 4, y: 4, z: 8, core: 2. Of those that a mesh axis runs over, the one named last changes fastest.
Arguments:
- activations: bfloat16 [16384, 3584], P(('group', 'ingroup')), may hold values from -6 to 6
- gate_weights: bfloat16 [256, 1792, 1024], P(('group', 'ingroup')), may hold values from -0.09375 to 0.09375
- up_weights: bfloat16 [256, 1792, 1024], P(('group', 'ingroup')), may hold values from -0.09375 to 0.09375
- down_weights: bfloat16 [256, 1024, 1792], P(('group', 'ingroup')), may hold values from -0.375 to 0.375
- expert_ids: int32 [16384, 8], P(('group', 'ingroup')), may hold values from 0 to 127, as said below
- gate_scores: int32 [16384, 8], P(('group', 'ingroup')), may hold values from 1 to 15
- arrival_pos: int32 [16384], P(('group', 'ingroup')), may hold values from 0 to 63, as said below
Outputs:
- expert_mix: bfloat16 [16384, 3584], P(('group', 'ingroup'))
Inputs may be any that keep to these rules, and one draw needn't show every extreme that they name: `expert_ids`: each row names 8 different experts, two from each of 4 different groups. Among one device's 64 rows no expert is named more than 6 times and no group by more than 24 rows; on every device some expert is named exactly 6 times and some group by exactly 24 rows. `arrival_pos`: within each device's 64 rows the values are a permutation.
All inputs are finite; a program needn't handle non-finite values.
Results may differ from a plain program's by a relative error of at most 0.0077.
Values may be sent and summed in bfloat16 or wider, within the bound.
No kernel may reach another device: no remote copies, remote signals or barrier semaphores. Data moves between devices by JAX's collectives and lax.ppermute only.
A program may use at most 128 MiB of HBM per device.

v0:
```python
import jax
import jax.numpy as jnp
from jax import lax
from jax.sharding import PartitionSpec as P

TOPG = 4


def from_partner(shard, axis, apart):
    return lax.ppermute(shard, axis, [(i, i ^ 1 << apart) for i in range(lax.axis_size(axis))])


def group_layout(int_table, groups, members, expert_most):
    shaped = int_table.reshape(groups, members // 2, 1, expert_most)
    shaped = jnp.broadcast_to(shaped, (groups, members // 2, 2, expert_most))
    return shaped.reshape(groups, members, expert_most)


def per_device(
    activations, gate_weights, up_weights, down_weights, expert_ids, gate_scores, arrival_pos
):
    groups = lax.axis_size("group")
    members = lax.axis_size("ingroup")
    per_group = members // 2
    experts = groups * per_group
    tok_count = activations.shape[0]
    model_width = activations.shape[1]
    half_width = model_width // 2
    top_picks = expert_ids.shape[1]
    capacity = 2 * top_picks * tok_count
    group_most = min(tok_count, 3 * tok_count * TOPG // (2 * groups))
    expert_most = (2 * group_most + per_group - 1) // per_group
    expert_range = jnp.arange(experts, dtype=jnp.int32)
    pick_hits = (expert_ids[:, :, None] == expert_range[None, None, :]).astype(jnp.int32)
    hit_table = jnp.sum(pick_hits, axis=1)
    occurrence = jnp.cumsum(hit_table, axis=0) - hit_table
    position_range = jnp.arange(tok_count, dtype=jnp.int32)
    arrival_table = (arrival_pos[:, None] == position_range[None, :]).astype(jnp.int32)
    own_counts = jnp.dot(hit_table.T, arrival_table)
    shifts = jnp.arange(32, dtype=jnp.int32)
    flat_bits = own_counts.reshape(-1, 32)
    packed = jnp.sum(jnp.left_shift(flat_bits, shifts[None, :]), axis=1)[None, :]
    my_index = lax.axis_index(("group", "ingroup"))
    piece = lax.all_gather(packed, ("group", "ingroup"), axis=0, tiled=True)
    bit_table = jnp.bitwise_and(jnp.right_shift(piece[:, :, None], shifts[None, None, :]), 1)
    bit_table = bit_table.reshape(piece.shape[0], experts, tok_count)
    source_index = jnp.arange(piece.shape[0], dtype=jnp.int32)
    earlier_flag = (source_index < my_index).astype(jnp.int32)
    prior_part = jnp.sum(bit_table * earlier_flag[:, None, None], axis=0)
    total_part = jnp.sum(bit_table, axis=0)
    earlier = jnp.cumsum(total_part, axis=1) - total_part
    rank_table = earlier + prior_part
    rank_by_token = jnp.dot(arrival_table, rank_table.T)
    pick_rank = jnp.sum(pick_hits * rank_by_token[:, None, :], axis=2)
    pick_occurrence = jnp.sum(pick_hits * occurrence[:, None, :], axis=2)
    kept_mask = (pick_rank < capacity).astype(jnp.int32)
    kept_scores = gate_scores * kept_mask
    weight_sum = jnp.maximum(jnp.sum(kept_scores, axis=1), 1)
    routing = kept_scores.astype(jnp.float32) / weight_sum.astype(jnp.float32)[:, None]
    slot_range = jnp.arange(expert_most, dtype=jnp.int32)
    slot_match = hit_table[:, :, None] * (
        occurrence[:, :, None] == slot_range[None, None, :]
    ).astype(jnp.int32)
    slot_valid = jnp.sum(slot_match, axis=0)
    slot_token = jnp.sum(slot_match * position_range[:, None, None], axis=0)
    slot_rank = jnp.sum(slot_match * rank_by_token[:, :, None], axis=0)
    send_rank = jnp.where((slot_valid > 0) & (slot_rank < capacity), slot_rank, -1)
    half_index = jnp.arange(members, dtype=jnp.int32) % 2
    token_layout = jnp.transpose(group_layout(slot_token, groups, members, expert_most), (1, 0, 2))
    rank_layout = jnp.transpose(group_layout(send_rank, groups, members, expert_most), (1, 0, 2))
    feature_rows = activations.reshape(tok_count * 2, half_width)
    send_rows = jnp.take(feature_rows, token_layout * 2 + half_index[:, None, None], axis=0)
    got_rows, got_rank = (
        lax.all_to_all(
            lax.all_to_all(send_rows, "group", split_axis=1, concat_axis=1, tiled=True),
            "ingroup",
            split_axis=0,
            concat_axis=0,
            tiled=True,
        ),
        lax.all_to_all(
            lax.all_to_all(rank_layout, "group", split_axis=1, concat_axis=1, tiled=True),
            "ingroup",
            split_axis=0,
            concat_axis=0,
            tiled=True,
        ),
    )
    slot_total = members * groups * expert_most
    flat_rank = got_rank.reshape(slot_total)
    flat_rows = got_rows.reshape(slot_total, half_width)
    target = jnp.where(flat_rank >= 0, flat_rank, capacity)
    source_of = (
        jnp.zeros((capacity,), jnp.int32)
        .at[target]
        .set(jnp.arange(slot_total, dtype=jnp.int32), mode="drop")
    )
    filled = jnp.zeros((capacity,), jnp.bool_).at[target].set(True, mode="drop")
    expert_rows = jnp.where(
        filled[:, None], jnp.take(flat_rows, source_of, axis=0), jnp.zeros((), activations.dtype)
    )
    gate_part = jnp.dot(expert_rows, gate_weights[0], preferred_element_type=jnp.float32).astype(
        jnp.bfloat16
    )
    up_part = jnp.dot(expert_rows, up_weights[0], preferred_element_type=jnp.float32).astype(
        jnp.bfloat16
    )
    other_gate, other_up = from_partner((gate_part, up_part), "ingroup", 0)
    gate_sum = gate_part.astype(jnp.float32) + other_gate.astype(jnp.float32)
    up_sum = up_part.astype(jnp.float32) + other_up.astype(jnp.float32)
    hidden = (jax.nn.silu(gate_sum) * up_sum).astype(jnp.bfloat16)
    expert_out = jnp.dot(hidden, down_weights[0], preferred_element_type=jnp.float32).astype(
        jnp.bfloat16
    )
    back_rows = jnp.take(expert_out, jnp.clip(flat_rank, 0, capacity - 1), axis=0)
    back_rows = jnp.where((flat_rank >= 0)[:, None], back_rows, jnp.zeros((), jnp.bfloat16))
    back_rows = back_rows.reshape(members, groups, expert_most, half_width)
    pick_group = expert_ids // per_group
    returned = lax.all_to_all(
        lax.all_to_all(back_rows, "group", split_axis=1, concat_axis=1, tiled=True),
        "ingroup",
        split_axis=0,
        concat_axis=0,
        tiled=True,
    )
    pick_member = expert_ids % per_group * 2
    halves = jnp.arange(2, dtype=jnp.int32)
    flat_pick = (
        (pick_member[:, :, None] + halves[None, None, :]) * groups + pick_group[:, :, None]
    ) * expert_most + pick_occurrence[:, :, None]
    gathered = jnp.take(returned.reshape(slot_total, half_width), flat_pick, axis=0)
    terms = routing[:, :, None] * gathered.reshape(tok_count, top_picks, model_width).astype(
        jnp.float32
    )
    pick_range = jnp.arange(top_picks, dtype=jnp.int32)
    not_self = (pick_range[:, None] != pick_range[None, :]).astype(jnp.int32)
    same_other = (pick_group[:, :, None] == pick_group[:, None, :]).astype(jnp.int32) * not_self[
        None, :, :
    ]
    partner = jnp.sum(same_other * pick_range[None, None, :], axis=2)
    partner_terms = jnp.take_along_axis(terms, partner[:, :, None], axis=1)
    paired = terms + partner_terms
    rounded = lax.optimization_barrier(paired.astype(jnp.bfloat16)).astype(jnp.float32)
    combined = 0.5 * jnp.sum(rounded, axis=1)
    return combined.astype(jnp.bfloat16)


def solution(mesh):
    return jax.shard_map(
        per_device,
        mesh=mesh,
        in_specs=(
            P(("group", "ingroup"), None),
            P(("group", "ingroup"), None, None),
            P(("group", "ingroup"), None, None),
            P(("group", "ingroup"), None, None),
            P(("group", "ingroup"), None),
            P(("group", "ingroup"), None),
            P(("group", "ingroup")),
        ),
        out_specs=P(("group", "ingroup"), None),
        check_vma=False,
    )
```

profile of v0, /device:TPU:1, one launch (start us, length us, event | category | flops | bytes accessed | tf_op | source)
XLA Modules:
  0.0 716.8 jit_solution(8007721992500397717)
XLA Ops:
  0.0 0.8 copy.125
  0.8 0.1 convert_reduce_fusion.1
  1.0 0.9 fusion.22
  2.0 0.1 shift-left_reduce_fusion
  2.1 67.0 %all-gather.1 = s32[256,1,256]{2,1,0:T(1,128)S(1)} all-gather(s32[1,1,256]{2,1,0:T(1,128)S(1)} %bitcast.53), channel_id=2, replica_groups=mesh['group'=16,'ingroup'=16] {'group','ingroup'}, dimensions={0}, use_global_device_ids=true | all-gather | bytes 263168 | tf_op jit(solution)/shard_map/all_gather | solution.py:44
  69.2 1.7 fusion
  71.2 0.1 reduce_window_sum.23
  71.7 0.9 fusion.19
  72.9 0.7 copy.142
  73.7 4.2 all-to-all-start
  78.3 0.2 copy.149
  78.4 0.1 reshape.254
  78.6 0.2 reshape.248
  78.8 6.7 gather_fusion
  85.5 9.6 %reshape.253 = bf16[16,16,6,1792]{3,2,1,0:T(8,128)(2,1)} reshape(bf16[1536,1792]{1,0:T(8,128)(2,1)} %gather_fusion) | data formatting | bytes 11010048 | tf_op jit(solution)/shard_map/jit(_take)/gather | solution.py:72
  95.1 0.2 copy.148
  95.3 4.0 broadcast_select_fusion
  99.3 5.5 copy.150
  104.8 6.7 all-to-all-start.2
  111.5 0.7 copy.143
  112.2 80.3 %all-to-all-done.2 = bf16[16,16,6,1792]{3,0,2,1:T(8,128)(2,1)} async-done(((bf16[16,16,6,1792]{3,0,2,1:T(8,128)(2,1)}), bf16[16,16,6,1792]{3,0,2,1:T(8,128)(2,1)}, u32[]{:S(2)}, u32[]{:S(2)}) %all-to-all-start.2) | async-done | bytes 5505056 | tf_op jit(solution)/shard_map/all_to_all | solution.py:75
  192.5 6.3 all-to-all-start.1
  198.8 7.9 %copy.151 = bf16[16,16,6,1792]{3,1,2,0:T(8,128)(2,1)} copy(bf16[16,16,6,1792]{3,0,2,1:T(8,128)(2,1)} %all-to-all-done.2) | data formatting | bytes 11010048 | tf_op jit(solution)/shard_map/all_to_all | solution.py:75
  206.7 7.2 %all-to-all-start.3 = ((bf16[16,16,6,1792]{3,1,2,0:T(8,128)(2,1)}), bf16[16,16,6,1792]{3,1,2,0:T(8,128)(2,1)}, u32[]{:S(2)}, u32[]{:S(2)}) async-start(bf16[16,16,6,1792]{3,1,2,0:T(8,128)(2,1)} %copy.151), calls=%async_computation.3 | async-start | bytes 11010048 | tf_op jit(solution)/shard_map/all_to_all | solution.py:74
  213.9 0.2 copy.146
  214.1 0.1 reshape.247
  214.3 6.2 scatter_custom_fusion.1
  220.5 11.6 %scatter_custom_fusion = pred[1024]{0:T(1024)(128)(4,1)S(1)} fusion(s32[1536]{0:T(1024)S(1)} %get-tuple-element.13, pred[1536]{0:T(1024)(128)(4,1)S(1)} %broadcast.331, pred[]{:T(512)} %constant.148.clone.1), kind=kCustom, calls=%fused_computation.100 | custom fusion | bytes 1025 | tf_op jit(solution)/shard_map/scatter | solution.py:98
  232.2 103.5 %all-to-all-done.3 = bf16[16,16,6,1792]{3,1,2,0:T(8,128)(2,1)} async-done(((bf16[16,16,6,1792]{3,1,2,0:T(8,128)(2,1)}), bf16[16,16,6,1792]{3,1,2,0:T(8,128)(2,1)}, u32[]{:S(2)}, u32[]{:S(2)}) %all-to-all-start.3) | async-done | bytes 5505056 | tf_op jit(solution)/shard_map/all_to_all | solution.py:74
  335.7 7.7 %copy.152 = bf16[16,16,6,1792]{3,2,1,0:T(8,128)(2,1)} copy(bf16[16,16,6,1792]{3,1,2,0:T(8,128)(2,1)} %all-to-all-done.3) | data formatting | bytes 11010048 | tf_op jit(solution)/shard_map/all_to_all | solution.py:74
  343.3 9.7 %reshape.249 = bf16[1536,1792]{1,0:T(8,128)(2,1)} reshape(bf16[16,16,6,1792]{3,2,1,0:T(8,128)(2,1)} %copy.152) | data formatting | bytes 11010048 | tf_op jit(solution)/shard_map/reshape | solution.py:91
  353.0 11.2 %gather_fusion.1 = bf16[1024,1792]{1,0:T(8,128)(2,1)} fusion(bf16[1536,1792]{1,0:T(8,128)(2,1)} %reshape.249, s32[1024]{0:T(1024)S(1)} %fusion.37), kind=kCustom, calls=%fused_computation.1 | custom fusion | bytes 7344128 | tf_op jit(solution)/shard_map/jit(_take)/gather | solution.py:100
  364.2 7.3 %fusion.10 = bf16[1024,1024]{1,0:T(8,128)(2,1)S(1)} fusion(bf16[1,1792,1024]{2,1,0:T(8,128)(2,1)} %param.8, bf16[1024,1792]{1,0:T(8,128)(2,1)} %gather_fusion.1, pred[1024]{0:T(1024)(128)(4,1)S(1)} %compare_and_fusion.3, pred[1024]{0:T(1024)(128)(4,1)S(1)} %scatter_custom_fusion), kind=kOutput, calls=%fused_computation.28 | convolution fusion | flops 3762814976 | bytes 9439232 | tf_op jit(solution)/shard_map/dot_general | solution.py:102
  371.5 1.0 collective-permute-start
  372.5 5.6 fusion.13
  378.1 0.2 collective-permute-start.1
  378.3 0.2 copy.144
  378.5 0.2 copy.145
  378.7 4.0 collective-permute-done.1
  382.7 10.9 %convolution_convert_fusion = bf16[1024,1792]{1,0:T(8,128)(2,1)} fusion(bf16[1,1024,1792]{2,1,0:T(8,128)(2,1)} %param.10, bf16[1024,1024]{1,0:T(8,128)(2,1)} %collective-permute-done.1, bf16[1024,1024]{1,0:T(8,128)(2,1)} %fusion.13, bf16[1024,1024]{1,0:T(8,128)(2,1)} %collective-permute-done, bf16[1024,1024]{1,0:T(8,128)(2,1)S(1)} %fusion.10), kind=kOutput, calls=%fused_computation.18 | convolution fusion | flops 3772514304 | bytes 15728640 | tf_op jit(solution)/shard_map/dot_general | solution.py:112
  393.6 13.9 %gather_fusion.2 = bf16[1536,1792]{1,0:T(8,128)(2,1)} fusion(bf16[1024,1792]{1,0:T(8,128)(2,1)} %convolution_convert_fusion, s32[2048]{0:T(1024)S(1)} %pad_clamp_fusion), kind=kCustom, calls=%fused_computation.2 | custom fusion | bytes 11016192 | tf_op jit(solution)/shard_map/jit(_take)/gather | solution.py:115
  407.5 9.6 %gather.25 = bf16[16,16,6,1792]{3,2,1,0:T(8,128)(2,1)} reshape(bf16[1536,1792]{1,0:T(8,128)(2,1)} %gather_fusion.2) | data formatting | bytes 11010048 | tf_op jit(solution)/shard_map/jit(_take)/gather | solution.py:115
  417.1 4.4 select_select_fusion
  421.5 3.0 copy.153
  424.5 69.9 %all_to_all.30 = bf16[16,16,6,1792]{3,0,2,1:T(8,128)(2,1)S(1)} all-to-all(bf16[16,16,6,1792]{3,0,2,1:T(8,128)(2,1)S(1)} %copy.153), channel_id=1, replica_groups=mesh['group'=16,'ingroup'=16] {'group'}, dimensions={1} | all-to-all | bytes 11010048 | tf_op jit(solution)/shard_map/all_to_all | solution.py:120
  494.4 5.4 copy.154
  499.8 6.2 all-to-all-start.5
  506.0 2.3 select_reduce_fusion.2
  508.6 0.3 compare_select_fusion
  508.9 0.2 reshape.278
  509.0 0.2 copy.140
  509.8 0.1 copy.160
  510.2 117.6 %all-to-all-done.5 = bf16[16,16,6,1792]{3,1,2,0:T(8,128)(2,1)} async-done(((bf16[16,16,6,1792]{3,1,2,0:T(8,128)(2,1)}), bf16[16,16,6,1792]{3,1,2,0:T(8,128)(2,1)}, u32[]{:S(2)}, u32[]{:S(2)}) %all-to-all-start.5) | async-done | bytes 5505056 | tf_op jit(solution)/shard_map/all_to_all | solution.py:119
  627.7 7.7 %copy.155 = bf16[16,16,6,1792]{3,2,1,0:T(8,128)(2,1)} copy(bf16[16,16,6,1792]{3,1,2,0:T(8,128)(2,1)} %all-to-all-done.5) | data formatting | bytes 11010048 | tf_op jit(solution)/shard_map/all_to_all | solution.py:119
  635.4 9.7 %reshape.250 = bf16[1536,1792]{1,0:T(8,128)(2,1)} reshape(bf16[16,16,6,1792]{3,2,1,0:T(8,128)(2,1)} %copy.155) | data formatting | bytes 11010048 | tf_op jit(solution)/shard_map/reshape | solution.py:131
  645.1 11.2 %gather_fusion.3 = bf16[1024,1792]{1,0:T(8,128)(2,1)} fusion(bf16[1536,1792]{1,0:T(8,128)(2,1)} %reshape.250, s32[1024]{0:T(1024)S(1)} %broadcast_clamp_fusion), kind=kCustom, calls=%fused_computation.3 | custom fusion | bytes 7344128 | tf_op jit(solution)/shard_map/jit(_take)/gather | solution.py:131
  656.3 8.6 %reshape.277 = bf16[64,8,2,1792]{3,2,1,0:T(2,128)(2,1)} reshape(bf16[1024,1792]{1,0:T(8,128)(2,1)} %gather_fusion.3) | data formatting | bytes 7340032 | tf_op jit(solution)/shard_map/jit(_take)/gather | solution.py:131
  664.9 8.5 %fusion.3 = f32[64,8,2,1792]{3,2,1,0:T(2,128)} fusion(bf16[64,8,2,1792]{3,2,1,0:T(2,128)(2,1)} %reshape.277, pred[64,8,2]{2,1,0:T(8,128)(4,1)S(1)} %copy.140), kind=kLoop, calls=%fused_computation.19 | loop fusion | flops 3670016 | bytes 11011072 | tf_op jit(solution)/shard_map/convert_element_type | solution.py:132
  673.4 10.0 %reshape.251 = f32[64,8,3584]{2,1,0:T(8,128)} reshape(f32[64,8,2,1792]{3,2,1,0:T(2,128)} %fusion.3) | data formatting | bytes 14680064 | tf_op jit(solution)/shard_map/convert_element_type | solution.py:132
  683.4 6.9 broadcast_multiply_fusion
  690.3 16.6 %gather_fusion.4 = f32[512,3584]{1,0:T(8,128)} fusion(f32[64,8,3584]{2,1,0:T(8,128)} %broadcast_multiply_fusion, s32[512]{0:T(512)S(1)} %reshape.284), kind=kCustom, calls=%fused_computation.4 | custom fusion | bytes 14684160 | tf_op jit(solution)/shard_map/jit(take_along_axis)/gather | solution.py:141
  706.9 6.2 fusion.2
  713.1 2.4 convert_reduce_fusion
  715.5 0.8 multiply_convert_fusion.2
  (63 shorter events, 2.6 us)
Async XLA Ops:
  0.0 78.6 %copy-start.1 = (bf16[64,3584]{1,0:T(8,128)(2,1)S(1)}, bf16[64,3584]{1,0:T(8,128)(2,1)}, u32[]{:S(2)}) copy-start(bf16[64,3584]{1,0:T(8,128)(2,1)} %param.7) | copy-start | bytes 1376260
  73.7 31.1 %all-to-all-start = ((s32[16,16,6]{0,2,1:T(8,128)}), s32[16,16,6]{0,2,1:T(8,128)S(1)}, u32[]{:S(2)}, u32[]{:S(2)}) async-start(s32[16,16,6]{0,2,1:T(8,128)} %copy.142), calls=%async_computation | async-start | bytes 131072 | tf_op jit(solution)/shard_map/all_to_all | solution.py:82
  104.8 87.7 %all-to-all-start.2 = ((bf16[16,16,6,1792]{3,0,2,1:T(8,128)(2,1)}), bf16[16,16,6,1792]{3,0,2,1:T(8,128)(2,1)}, u32[]{:S(2)}, u32[]{:S(2)}) async-start(bf16[16,16,6,1792]{3,0,2,1:T(8,128)(2,1)} %copy.150), calls=%async_computation.2 | async-start | bytes 11010048 | tf_op jit(solution)/shard_map/all_to_all | solution.py:75
  192.5 14.2 %all-to-all-start.1 = ((s32[16,16,6]{1,2,0:T(8,128)}), s32[16,16,6]{1,2,0:T(8,128)S(1)}, u32[]{:S(2)}, u32[]{:S(2)}) async-start(s32[16,16,6]{1,2,0:T(8,128)} %copy.143), calls=%async_computation.1 | async-start | bytes 131072 | tf_op jit(solution)/shard_map/all_to_all | solution.py:81
  206.7 129.0 %all-to-all-start.3 = ((bf16[16,16,6,1792]{3,1,2,0:T(8,128)(2,1)}), bf16[16,16,6,1792]{3,1,2,0:T(8,128)(2,1)}, u32[]{:S(2)}, u32[]{:S(2)}) async-start(bf16[16,16,6,1792]{3,1,2,0:T(8,128)(2,1)} %copy.151), calls=%async_computation.3 | async-start | bytes 11010048 | tf_op jit(solution)/shard_map/all_to_all | solution.py:74
  364.2 8.3 %copy-start = (bf16[1024,1792]{1,0:T(8,128)(2,1)S(1)}, bf16[1024,1792]{1,0:T(8,128)(2,1)}, u32[]{:S(2)}) copy-start(bf16[1024,1792]{1,0:T(8,128)(2,1)} %gather_fusion.1) | copy-start | bytes 11010052
  364.2 8.3 %copy-start.3 = (bf16[1,1792,1024]{2,1,0:T(8,128)(2,1)S(1)}, bf16[1,1792,1024]{2,1,0:T(8,128)(2,1)}, u32[]{:S(2)}) copy-start(bf16[1,1792,1024]{2,1,0:T(8,128)(2,1)} %param.9) | copy-start | bytes 11010052
  371.5 7.2 %collective-permute-start = (bf16[1024,1024]{1,0:T(8,128)(2,1)S(1)}, bf16[1024,1024]{1,0:T(8,128)(2,1)}, u32[]{:S(2)}, u32[]{:S(2)}) collective-permute-start(bf16[1024,1024]{1,0:T(8,128)(2,1)S(1)} %fusion.10), channel_id=1, source_target_pairs={{0,1},{1,0},{2,3},{3,2},{4,5},{5,4},{6,7},{7,6},{8,9},{9,8},{10,11... | collective-permute-start | bytes 6291464 | tf_op jit(solution)/shard_map/ppermute | solution.py:10
  378.1 4.7 collective-permute-start.1
  499.8 9.5 %copy-start.2 = (s32[64,8]{0,1:T(8,128)S(1)}, s32[64,8]{0,1:T(8,128)}, u32[]{:S(2)}) copy-start(s32[64,8]{0,1:T(8,128)} %param.12) | copy-start | bytes 6148
  499.8 128.0 %all-to-all-start.5 = ((bf16[16,16,6,1792]{3,1,2,0:T(8,128)(2,1)}), bf16[16,16,6,1792]{3,1,2,0:T(8,128)(2,1)}, u32[]{:S(2)}, u32[]{:S(2)}) async-start(bf16[16,16,6,1792]{3,1,2,0:T(8,128)(2,1)} %copy.154), calls=%async_computation.5 | async-start | bytes 11010048 | tf_op jit(solution)/shard_map/all_to_all | solution.py:119
where the time goes:
time: 726 us; the launch traced here: 717 us
  waiting for transfers between devices  305 us (42%)
  local copies, waits for them, and re-layouts  177 us (24%)
  blocking collectives  137 us (19%)
  other arithmetic  38.8 us (5%)
  starting transfers between devices  31.8 us (4%)
  matrix products  25.6 us (4%)
    all_to_all x1, waiting for transfers between devices, per_device(): lax.all_to_all(lax.all_to_all(back_rows, 'group', split_axis=1, concat_ax...  118 us
    all_to_all x1, waiting for transfers between devices, per_device(): lax.all_to_all(lax.all_to_all(send_rows, 'group', split_axis=1, concat_ax...  104 us
    all_to_all x1, waiting for transfers between devices, per_device(): lax.all_to_all(send_rows, 'group', split_axis=1, concat_axis=1, tiled=True)  80.3 us
    all_to_all x1, blocking collectives, per_device(): lax.all_to_all(back_rows, 'group', split_axis=1, concat_axis=1, tiled=True)  69.9 us
    all_gather x1, blocking collectives, per_device(): piece = lax.all_gather(packed, ('group', 'ingroup'), axis=0, tiled=True)  67 us
    gather x2, local copies, waits for them, and re-layouts, per_device(): jnp.take(expert_out, jnp.clip(flat_rank, 0, capacity - 1), axis=0)  23.4 us
    gather x2, local copies, waits for them, and re-layouts, per_device(): jnp.take(returned.reshape(slot_total, half_width), flat_pick, axis=0)  19.8 us
    gather x3, local copies, waits for them, and re-layouts, per_device(): partner_terms = jnp.take_along_axis(terms, partner[:, :, None], axis=1)  16.8 us
  transfers between devices with their start and end apart: 7, of which 4 were waited for; matrix products, arithmetic and copies ran while one was open for 9% of the time, Pallas kernels for 0%

commit v1 on v0

--- a/solution.py
+++ b/solution.py
@@ -4,6 +4,22 @@
 from jax.sharding import PartitionSpec as P
 
 TOPG = 4
+
+
+def pairwise_exchange(array, axis, split, join):
+    ways, here = (lax.axis_size(axis), lax.axis_index(axis))
+    width = array.shape[split] // ways
+    dims = list(array.shape)
+    dims[split] = width
+    height = dims[join]
+    dims[join] = height * ways
+    full = jnp.zeros(dims, array.dtype)
+    for mask in range(ways):
+        part = lax.dynamic_slice_in_dim(array, (here ^ mask) * width, width, axis=split)
+        if mask:
+            part = lax.ppermute(part, axis, [(d, d ^ mask) for d in range(ways)])
+        full = lax.dynamic_update_slice_in_dim(full, part, (here ^ mask) * height, axis=join)
+    return full
 
 
 def from_partner(shard, axis, apart):
@@ -117,7 +133,7 @@
     back_rows = back_rows.reshape(members, groups, expert_most, half_width)
     pick_group = expert_ids // per_group
     returned = lax.all_to_all(
-        lax.all_to_all(back_rows, "group", split_axis=1, concat_axis=1, tiled=True),
+        pairwise_exchange(back_rows, "group", 1, 1),
         "ingroup",
         split_axis=0,
         concat_axis=0,

time: 726 us -> 786 us (1.083)
  waiting for transfers between devices: 305 us -> 407 us
  blocking collectives: 137 us -> 67 us
  starting transfers between devices: 31.8 us -> 59.7 us
    ppermute x0 -> x15, waiting for transfers between devices: none -> 101 us  [pairwise_exchange(): part = lax.ppermute(part, axis, [(d, d ^ mask) for d in range(ways)])]
    all_to_all x1 -> x0, blocking collectives: 69.9 us -> none  [per_device(): lax.all_to_all(back_rows, 'group', split_axis=1, concat_axis=1, tiled=True)]
    ppermute x0 -> x15, starting transfers between devices: none -> 28.4 us  [pairwise_exchange(): part = lax.ppermute(part, axis, [(d, d ^ mask) for d in range(ways)])]
  transfers between devices with their start and end apart: 7 -> 22, of which waited for: 4 -> 11; matrix products, arithmetic and copies ran while one was open for 9% -> 8% of each run, Pallas kernels for 0% -> 0%
where the time goes in v1:
time: 786 us; the launch traced here: 777 us
  waiting for transfers between devices  407 us (52%)
  local copies, waits for them, and re-layouts  176 us (22%)
  blocking collectives  67 us (9%)
  starting transfers between devices  59.7 us (8%)
  other arithmetic  38.8 us (5%)
  matrix products  27.5 us (3%)
    all_to_all x1, waiting for transfers between devices, per_device(): lax.all_to_all(pairwise_exchange(back_rows, 'group', 1, 1), 'ingroup', sp...  117 us
    all_to_all x1, waiting for transfers between devices, per_device(): lax.all_to_all(lax.all_to_all(send_rows, 'group', split_axis=1, concat_ax...  104 us
    ppermute x15, waiting for transfers between devices, pairwise_exchange(): part = lax.ppermute(part, axis, [(d, d ^ mask) for d in range(ways)])  101 us
    all_to_all x1, waiting for transfers between devices, per_device(): lax.all_to_all(send_rows, 'group', split_axis=1, concat_axis=1, tiled=True)  80.3 us
    all_gather x1, blocking collectives, per_device(): piece = lax.all_gather(packed, ('group', 'ingroup'), axis=0, tiled=True)  67 us
    ppermute x15, starting transfers between devices, pairwise_exchange(): part = lax.ppermute(part, axis, [(d, d ^ mask) for d in range(ways)])  28.4 us
    gather x2, local copies, waits for them, and re-layouts, per_device(): jnp.take(expert_out, jnp.clip(flat_rank, 0, capacity - 1), axis=0)  23.4 us
    gather x2, local copies, waits for them, and re-layouts, per_device(): jnp.take(returned.reshape(slot_total, half_width), flat_pick, axis=0)  19.7 us
  transfers between devices with their start and end apart: 22, of which 11 were waited for; matrix products, arithmetic and copies ran while one was open for 8% of the time, Pallas kernels for 0%

profile of v1, /device:TPU:1, one launch (start us, length us, event | category | flops | bytes accessed | tf_op | source)
XLA Modules:
  0.0 776.7 jit_solution(5417043176943327743)
XLA Ops:
  0.0 0.8 copy.122
  0.9 0.9 fusion.22
  2.1 67.0 %all-gather.1 = s32[256,1,256]{2,1,0:T(1,128)S(1)} all-gather(s32[1,1,256]{2,1,0:T(1,128)S(1)} %bitcast.53), channel_id=2, replica_groups=mesh['group'=16,'ingroup'=16] {'group','ingroup'}, dimensions={0}, use_global_device_ids=true | all-gather | bytes 263168 | tf_op jit(solution)/shard_map/all_gather | solution.py:60
  69.1 1.7 fusion
  71.6 0.9 fusion.19
  73.6 4.2 all-to-all-start
  78.5 1.2 reshape.248
  79.7 6.7 gather_fusion
  86.5 9.6 %reshape.253 = bf16[16,16,6,1792]{3,2,1,0:T(8,128)(2,1)} reshape(bf16[1536,1792]{1,0:T(8,128)(2,1)} %gather_fusion) | data formatting | bytes 11010048 | tf_op jit(solution)/shard_map/jit(_take)/gather | solution.py:88
  96.2 4.0 broadcast_select_fusion
  100.2 5.5 copy.147
  105.7 6.7 all-to-all-start.2
  112.4 0.7 copy.140
  113.1 80.3 %all-to-all-done.2 = bf16[16,16,6,1792]{3,0,2,1:T(8,128)(2,1)} async-done(((bf16[16,16,6,1792]{3,0,2,1:T(8,128)(2,1)}), bf16[16,16,6,1792]{3,0,2,1:T(8,128)(2,1)}, u32[]{:S(2)}, u32[]{:S(2)}) %all-to-all-start.2) | async-done | bytes 5505056 | tf_op jit(solution)/shard_map/all_to_all | solution.py:91
  193.4 6.5 all-to-all-start.1
  200.0 7.9 %copy.148 = bf16[16,16,6,1792]{3,1,2,0:T(8,128)(2,1)} copy(bf16[16,16,6,1792]{3,0,2,1:T(8,128)(2,1)} %all-to-all-done.2) | data formatting | bytes 11010048 | tf_op jit(solution)/shard_map/all_to_all | solution.py:91
  207.9 7.2 all-to-all-start.3
  215.5 6.2 scatter_custom_fusion.1
  221.7 11.4 %scatter_custom_fusion = pred[1024]{0:T(1024)(128)(4,1)S(1)} fusion(s32[1536]{0:T(1024)S(1)} %get-tuple-element.13, pred[1536]{0:T(1024)(128)(4,1)S(1)} %broadcast.331, pred[]{:T(512)} %constant.163.clone.1), kind=kCustom, calls=%fused_computation.131 | custom fusion | bytes 1025 | tf_op jit(solution)/shard_map/scatter | solution.py:114
  233.1 103.7 %all-to-all-done.3 = bf16[16,16,6,1792]{3,1,2,0:T(8,128)(2,1)} async-done(((bf16[16,16,6,1792]{3,1,2,0:T(8,128)(2,1)}), bf16[16,16,6,1792]{3,1,2,0:T(8,128)(2,1)}, u32[]{:S(2)}, u32[]{:S(2)}) %all-to-all-start.3) | async-done | bytes 5505056 | tf_op jit(solution)/shard_map/all_to_all | solution.py:90
  336.8 7.7 copy.149
  344.5 9.7 %reshape.249 = bf16[1536,1792]{1,0:T(8,128)(2,1)} reshape(bf16[16,16,6,1792]{3,2,1,0:T(8,128)(2,1)} %copy.149) | data formatting | bytes 11010048 | tf_op jit(solution)/shard_map/reshape | solution.py:107
  354.2 11.2 %gather_fusion.1 = bf16[1024,1792]{1,0:T(8,128)(2,1)} fusion(bf16[1536,1792]{1,0:T(8,128)(2,1)} %reshape.249, s32[1024]{0:T(1024)S(1)} %fusion.37), kind=kCustom, calls=%fused_computation.1 | custom fusion | bytes 7344128 | tf_op jit(solution)/shard_map/jit(_take)/gather | solution.py:116
  365.4 8.6 %fusion.10 = bf16[1024,1024]{1,0:T(8,128)(2,1)} fusion(bf16[1,1792,1024]{2,1,0:T(8,128)(2,1)} %param.8, bf16[1024,1792]{1,0:T(8,128)(2,1)} %gather_fusion.1, pred[1024]{0:T(1024)(128)(4,1)S(1)} %compare_and_fusion.3, pred[1024]{0:T(1024)(128)(4,1)S(1)} %scatter_custom_fusion), kind=kOutput, calls=%fused_computation.28 | convolution fusion | flops 3762814976 | bytes 9439232 | tf_op jit(solution)/shard_map/dot_general | solution.py:118
  374.0 0.9 collective-permute-start
  374.9 5.7 fusion.13
  381.3 3.9 collective-permute-done.1
  385.3 11.4 %convolution_convert_fusion = bf16[1024,1792]{1,0:T(8,128)(2,1)} fusion(bf16[1,1024,1792]{2,1,0:T(8,128)(2,1)} %param.10, bf16[1024,1024]{1,0:T(8,128)(2,1)} %collective-permute-done.1, bf16[1024,1024]{1,0:T(8,128)(2,1)} %fusion.13, bf16[1024,1024]{1,0:T(8,128)(2,1)} %collective-permute-done, bf16[1024,1024]{1,0:T(8,128)(2,1)} %fusion.10), kind=kOutput, calls=%fused_computation.18 | convolution fusion | flops 3772514304 | bytes 15728640 | tf_op jit(solution)/shard_map/dot_general | solution.py:128
  396.7 13.9 %gather_fusion.2 = bf16[1536,1792]{1,0:T(8,128)(2,1)} fusion(bf16[1024,1792]{1,0:T(8,128)(2,1)} %convolution_convert_fusion, s32[2048]{0:T(1024)S(1)} %pad_clamp_fusion), kind=kCustom, calls=%fused_computation.2 | custom fusion | bytes 11016192 | tf_op jit(solution)/shard_map/jit(_take)/gather | solution.py:131
  410.6 9.6 %gather.25 = bf16[16,16,6,1792]{3,2,1,0:T(8,128)(2,1)} reshape(bf16[1536,1792]{1,0:T(8,128)(2,1)} %gather_fusion.2) | data formatting | bytes 11010048 | tf_op jit(solution)/shard_map/jit(_take)/gather | solution.py:131
  420.1 4.4 select_select_fusion
  425.2 1.0 constant_dynamic-slice_fusion
  426.3 2.4 collective-permute-start.3
  428.7 1.5 collective-permute-start.4
  430.6 7.7 collective-permute-done.2
  438.3 1.3 collective-permute-start.7
  439.6 9.4 %collective-permute-done.3 = bf16[16,1,6,1792]{3,2,1,0:T(8,128)(2,1)S(1)} collective-permute-done((bf16[16,1,6,1792]{3,2,1,0:T(8,128)(2,1)S(1)}, bf16[16,1,6,1792]{3,2,1,0:T(8,128)(2,1)S(1)}, u32[]{:S(2)}, u32[]{:S(2)}) %collective-permute-start.3) | collective-permute-done | bytes 344096 | tf_op jit(solution)/shard_map/ppermute | solution.py:20
  449.1 1.6 collective-permute-start.8
  451.1 2.7 collective-permute-start.9
  454.0 10.0 %collective-permute-done.6 = bf16[16,1,6,1792]{3,2,1,0:T(8,128)(2,1)S(1)} collective-permute-done((bf16[16,1,6,1792]{3,2,1,0:T(8,128)(2,1)S(1)}, bf16[16,1,6,1792]{3,2,1,0:T(8,128)(2,1)S(1)}, u32[]{:S(2)}, u32[]{:S(2)}) %collective-permute-start.6) | collective-permute-done | bytes 344096 | tf_op jit(solution)/shard_map/ppermute | solution.py:20
  464.0 4.0 collective-permute-start.11
  468.1 7.0 collective-permute-done.7
  475.1 4.2 collective-permute-start.12
  479.3 1.9 collective-permute-start.13
  481.3 36.3 %collective-permute-done.9 = bf16[16,1,6,1792]{3,2,1,0:T(8,128)(2,1)S(1)} collective-permute-done((bf16[16,1,6,1792]{3,2,1,0:T(8,128)(2,1)S(1)}, bf16[16,1,6,1792]{3,2,1,0:T(8,128)(2,1)S(1)}, u32[]{:S(2)}, u32[]{:S(2)}) %collective-permute-start.9) | collective-permute-done | bytes 344096 | tf_op jit(solution)/shard_map/ppermute | solution.py:20
  517.6 2.1 collective-permute-start.14
  519.8 4.7 collective-permute-start.15
  524.6 1.4 collective-permute-start.16
  526.1 30.7 %collective-permute-done.13 = bf16[16,1,6,1792]{3,2,1,0:T(8,128)(2,1)S(1)} collective-permute-done((bf16[16,1,6,1792]{3,2,1,0:T(8,128)(2,1)S(1)}, bf16[16,1,6,1792]{3,2,1,0:T(8,128)(2,1)S(1)}, u32[]{:S(2)}, u32[]{:S(2)}) %collective-permute-start.13) | collective-permute-done | bytes 344096 | tf_op jit(solution)/shard_map/ppermute | solution.py:20
  557.2 3.7 copy.150
  560.9 5.5 all-to-all-start.4
  566.4 2.3 select_reduce_fusion.2
  570.5 117.4 %all-to-all-done.4 = bf16[16,16,6,1792]{3,1,2,0:T(8,128)(2,1)} async-done(((bf16[16,16,6,1792]{3,1,2,0:T(8,128)(2,1)}), bf16[16,16,6,1792]{3,1,2,0:T(8,128)(2,1)}, u32[]{:S(2)}, u32[]{:S(2)}) %all-to-all-start.4) | async-done | bytes 5505056 | tf_op jit(solution)/shard_map/all_to_all | solution.py:135
  688.0 7.7 copy.151
  695.7 9.7 %reshape.250 = bf16[1536,1792]{1,0:T(8,128)(2,1)} reshape(bf16[16,16,6,1792]{3,2,1,0:T(8,128)(2,1)} %copy.151) | data formatting | bytes 11010048 | tf_op jit(solution)/shard_map/reshape | solution.py:147
  705.3 11.2 %gather_fusion.3 = bf16[1024,1792]{1,0:T(8,128)(2,1)} fusion(bf16[1536,1792]{1,0:T(8,128)(2,1)} %reshape.250, s32[1024]{0:T(1024)S(1)} %broadcast_clamp_fusion), kind=kCustom, calls=%fused_computation.3 | custom fusion | bytes 7344128 | tf_op jit(solution)/shard_map/jit(_take)/gather | solution.py:147
  716.5 8.5 %reshape.277 = bf16[64,8,2,1792]{3,2,1,0:T(2,128)(2,1)} reshape(bf16[1024,1792]{1,0:T(8,128)(2,1)} %gather_fusion.3) | data formatting | bytes 7340032 | tf_op jit(solution)/shard_map/jit(_take)/gather | solution.py:147
  725.0 8.5 %fusion.3 = f32[64,8,2,1792]{3,2,1,0:T(2,128)} fusion(bf16[64,8,2,1792]{3,2,1,0:T(2,128)(2,1)} %reshape.277, pred[64,8,2]{2,1,0:T(8,128)(4,1)S(1)} %copy.137), kind=kLoop, calls=%fused_computation.19 | loop fusion | flops 3670016 | bytes 11011072 | tf_op jit(solution)/shard_map/convert_element_type | solution.py:148
  733.6 10.0 %reshape.251 = f32[64,8,3584]{2,1,0:T(8,128)} reshape(f32[64,8,2,1792]{3,2,1,0:T(2,128)} %fusion.3) | data formatting | bytes 14680064 | tf_op jit(solution)/shard_map/convert_element_type | solution.py:148
  743.6 6.9 broadcast_multiply_fusion
  750.4 16.6 %gather_fusion.4 = f32[512,3584]{1,0:T(8,128)} fusion(f32[64,8,3584]{2,1,0:T(8,128)} %broadcast_multiply_fusion, s32[512]{0:T(512)S(1)} %reshape.284), kind=kCustom, calls=%fused_computation.4 | custom fusion | bytes 14684160 | tf_op jit(solution)/shard_map/jit(take_along_axis)/gather | solution.py:157
  767.1 6.2 fusion.2
  773.2 2.4 convert_reduce_fusion
  775.7 0.8 multiply_convert_fusion.2
  (106 shorter events, 8.4 us)
Async XLA Ops:
  73.6 32.1 %all-to-all-start = ((s32[16,16,6]{0,2,1:T(8,128)}), s32[16,16,6]{0,2,1:T(8,128)S(1)}, u32[]{:S(2)}, u32[]{:S(2)}) async-start(s32[16,16,6]{0,2,1:T(8,128)} %copy.139), calls=%async_computation | async-start | bytes 131072 | tf_op jit(solution)/shard_map/all_to_all | solution.py:98
  105.7 87.7 %all-to-all-start.2 = ((bf16[16,16,6,1792]{3,0,2,1:T(8,128)(2,1)}), bf16[16,16,6,1792]{3,0,2,1:T(8,128)(2,1)}, u32[]{:S(2)}, u32[]{:S(2)}) async-start(bf16[16,16,6,1792]{3,0,2,1:T(8,128)(2,1)} %copy.147), calls=%async_computation.2 | async-start | bytes 11010048 | tf_op jit(solution)/shard_map/all_to_all | solution.py:91
  193.4 14.4 %all-to-all-start.1 = ((s32[16,16,6]{1,2,0:T(8,128)}), s32[16,16,6]{1,2,0:T(8,128)S(1)}, u32[]{:S(2)}, u32[]{:S(2)}) async-start(s32[16,16,6]{1,2,0:T(8,128)} %copy.140), calls=%async_computation.1 | async-start | bytes 131072 | tf_op jit(solution)/shard_map/all_to_all | solution.py:97
  207.9 129.0 %all-to-all-start.3 = ((bf16[16,16,6,1792]{3,1,2,0:T(8,128)(2,1)}), bf16[16,16,6,1792]{3,1,2,0:T(8,128)(2,1)}, u32[]{:S(2)}, u32[]{:S(2)}) async-start(bf16[16,16,6,1792]{3,1,2,0:T(8,128)(2,1)} %copy.148), calls=%async_computation.3 | async-start | bytes 11010048 | tf_op jit(solution)/shard_map/all_to_all | solution.py:90
  365.4 9.5 %copy-start = (bf16[1024,1792]{1,0:T(8,128)(2,1)S(1)}, bf16[1024,1792]{1,0:T(8,128)(2,1)}, u32[]{:S(2)}) copy-start(bf16[1024,1792]{1,0:T(8,128)(2,1)} %gather_fusion.1) | copy-start | bytes 11010052
  365.4 9.5 %copy-start.2 = (bf16[1,1792,1024]{2,1,0:T(8,128)(2,1)S(1)}, bf16[1,1792,1024]{2,1,0:T(8,128)(2,1)}, u32[]{:S(2)}) copy-start(bf16[1,1792,1024]{2,1,0:T(8,128)(2,1)} %param.9) | copy-start | bytes 11010052
  374.0 7.3 collective-permute-start
  380.6 4.7 collective-permute-start.1
  426.2 12.1 %collective-permute-start.2 = (bf16[16,1,6,1792]{3,2,1,0:T(8,128)(2,1)S(1)}, bf16[16,1,6,1792]{3,2,1,0:T(8,128)(2,1)S(1)}, u32[]{:S(2)}, u32[]{:S(2)}) collective-permute-start(bf16[16,1,6,1792]{3,2,1,0:T(8,128)(2,1)S(1)} %get-tuple-element.28), channel_id=1, source_target_pairs={{0,16},{16,0},{32,48},{48,32},{64,80},{80,64},{96,112},{112,96},{1... | collective-permute-start | bytes 1032200 | tf_op jit(solution)/shard_map/ppermute | solution.py:20
  426.3 22.7 %collective-permute-start.3 = (bf16[16,1,6,1792]{3,2,1,0:T(8,128)(2,1)S(1)}, bf16[16,1,6,1792]{3,2,1,0:T(8,128)(2,1)S(1)}, u32[]{:S(2)}, u32[]{:S(2)}) collective-permute-start(bf16[16,1,6,1792]{3,2,1,0:T(8,128)(2,1)S(1)} %get-tuple-element.27), channel_id=1, source_target_pairs={{0,32},{16,48},{32,0},{48,16},{64,96},{80,112},{96,64},{112,80},{1... | collective-permute-start | bytes 1032200 | tf_op jit(solution)/shard_map/ppermute | solution.py:20
  428.7 22.4 %collective-permute-start.4 = (bf16[16,1,6,1792]{3,2,1,0:T(8,128)(2,1)S(1)}, bf16[16,1,6,1792]{3,2,1,0:T(8,128)(2,1)S(1)}, u32[]{:S(2)}, u32[]{:S(2)}) collective-permute-start(bf16[16,1,6,1792]{3,2,1,0:T(8,128)(2,1)S(1)} %get-tuple-element.26), channel_id=1, source_target_pairs={{0,48},{16,32},{32,16},{48,0},{64,112},{80,96},{96,80},{112,64},{1... | collective-permute-start | bytes 1032200 | tf_op jit(solution)/shard_map/ppermute | solution.py:20
  430.2 23.7 %collective-permute-start.5 = (bf16[16,1,6,1792]{3,2,1,0:T(8,128)(2,1)S(1)}, bf16[16,1,6,1792]{3,2,1,0:T(8,128)(2,1)S(1)}, u32[]{:S(2)}, u32[]{:S(2)}) collective-permute-start(bf16[16,1,6,1792]{3,2,1,0:T(8,128)(2,1)S(1)} %get-tuple-element.25), channel_id=1, source_target_pairs={{0,64},{16,80},{32,96},{48,112},{64,0},{80,16},{96,32},{112,48},{1... | collective-permute-start | bytes 1032200 | tf_op jit(solution)/shard_map/ppermute | solution.py:20
  430.6 33.5 %collective-permute-start.6 = (bf16[16,1,6,1792]{3,2,1,0:T(8,128)(2,1)S(1)}, bf16[16,1,6,1792]{3,2,1,0:T(8,128)(2,1)S(1)}, u32[]{:S(2)}, u32[]{:S(2)}) collective-permute-start(bf16[16,1,6,1792]{3,2,1,0:T(8,128)(2,1)S(1)} %get-tuple-element.24), channel_id=1, source_target_pairs={{0,80},{16,64},{32,112},{48,96},{64,16},{80,0},{96,48},{112,32},{1... | collective-permute-start | bytes 1032200 | tf_op jit(solution)/shard_map/ppermute | solution.py:20
  438.3 36.8 %collective-permute-start.7 = (bf16[16,1,6,1792]{3,2,1,0:T(8,128)(2,1)S(1)}, bf16[16,1,6,1792]{3,2,1,0:T(8,128)(2,1)S(1)}, u32[]{:S(2)}, u32[]{:S(2)}) collective-permute-start(bf16[16,1,6,1792]{3,2,1,0:T(8,128)(2,1)S(1)} %get-tuple-element.23), channel_id=1, source_target_pairs={{0,96},{16,112},{32,64},{48,80},{64,32},{80,48},{96,0},{112,16},{1... | collective-permute-start | bytes 1032200 | tf_op jit(solution)/shard_map/ppermute | solution.py:20
  449.1 30.2 %collective-permute-start.8 = (bf16[16,1,6,1792]{3,2,1,0:T(8,128)(2,1)S(1)}, bf16[16,1,6,1792]{3,2,1,0:T(8,128)(2,1)S(1)}, u32[]{:S(2)}, u32[]{:S(2)}) collective-permute-start(bf16[16,1,6,1792]{3,2,1,0:T(8,128)(2,1)S(1)} %get-tuple-element.22), channel_id=1, source_target_pairs={{0,112},{16,96},{32,80},{48,64},{64,48},{80,32},{96,16},{112,0},{1... | collective-permute-start | bytes 1032200 | tf_op jit(solution)/shard_map/ppermute | solution.py:20
  451.1 66.5 %collective-permute-start.9 = (bf16[16,1,6,1792]{3,2,1,0:T(8,128)(2,1)S(1)}, bf16[16,1,6,1792]{3,2,1,0:T(8,128)(2,1)S(1)}, u32[]{:S(2)}, u32[]{:S(2)}) collective-permute-start(bf16[16,1,6,1792]{3,2,1,0:T(8,128)(2,1)S(1)} %get-tuple-element.21), channel_id=1, source_target_pairs={{0,128},{16,144},{32,160},{48,176},{64,192},{80,208},{96,224},{112... | collective-permute-start | bytes 1032200 | tf_op jit(solution)/shard_map/ppermute | solution.py:20
  453.9 65.9 %collective-permute-start.10 = (bf16[16,1,6,1792]{3,2,1,0:T(8,128)(2,1)S(1)}, bf16[16,1,6,1792]{3,2,1,0:T(8,128)(2,1)S(1)}, u32[]{:S(2)}, u32[]{:S(2)}) collective-permute-start(bf16[16,1,6,1792]{3,2,1,0:T(8,128)(2,1)S(1)} %get-tuple-element.20), channel_id=1, source_target_pairs={{0,144},{16,128},{32,176},{48,160},{64,208},{80,192},{96,240},{112... | collective-permute-start | bytes 1032200 | tf_op jit(solution)/shard_map/ppermute | solution.py:20
  464.0 60.6 %collective-permute-start.11 = (bf16[16,1,6,1792]{3,2,1,0:T(8,128)(2,1)S(1)}, bf16[16,1,6,1792]{3,2,1,0:T(8,128)(2,1)S(1)}, u32[]{:S(2)}, u32[]{:S(2)}) collective-permute-start(bf16[16,1,6,1792]{3,2,1,0:T(8,128)(2,1)S(1)} %get-tuple-element.19), channel_id=1, source_target_pairs={{0,160},{16,176},{32,128},{48,144},{64,224},{80,240},{96,192},{112... | collective-permute-start | bytes 1032200 | tf_op jit(solution)/shard_map/ppermute | solution.py:20
  475.1 51.0 %collective-permute-start.12 = (bf16[16,1,6,1792]{3,2,1,0:T(8,128)(2,1)S(1)}, bf16[16,1,6,1792]{3,2,1,0:T(8,128)(2,1)S(1)}, u32[]{:S(2)}, u32[]{:S(2)}) collective-permute-start(bf16[16,1,6,1792]{3,2,1,0:T(8,128)(2,1)S(1)} %get-tuple-element.18), channel_id=1, source_target_pairs={{0,176},{16,160},{32,144},{48,128},{64,240},{80,224},{96,208},{112... | collective-permute-start | bytes 1032200 | tf_op jit(solution)/shard_map/ppermute | solution.py:20
  479.3 77.6 %collective-permute-start.13 = (bf16[16,1,6,1792]{3,2,1,0:T(8,128)(2,1)S(1)}, bf16[16,1,6,1792]{3,2,1,0:T(8,128)(2,1)S(1)}, u32[]{:S(2)}, u32[]{:S(2)}) collective-permute-start(bf16[16,1,6,1792]{3,2,1,0:T(8,128)(2,1)S(1)} %get-tuple-element.17), channel_id=1, source_target_pairs={{0,192},{16,208},{32,224},{48,240},{64,128},{80,144},{96,160},{112... | collective-permute-start | bytes 1032200 | tf_op jit(solution)/shard_map/ppermute | solution.py:20
  517.6 39.3 %collective-permute-start.14 = (bf16[16,1,6,1792]{3,2,1,0:T(8,128)(2,1)S(1)}, bf16[16,1,6,1792]{3,2,1,0:T(8,128)(2,1)S(1)}, u32[]{:S(2)}, u32[]{:S(2)}) collective-permute-start(bf16[16,1,6,1792]{3,2,1,0:T(8,128)(2,1)S(1)} %get-tuple-element.16), channel_id=1, source_target_pairs={{0,208},{16,192},{32,240},{48,224},{64,144},{80,128},{96,176},{112... | collective-permute-start | bytes 1032200 | tf_op jit(solution)/shard_map/ppermute | solution.py:20
  519.8 37.2 %collective-permute-start.15 = (bf16[16,1,6,1792]{3,2,1,0:T(8,128)(2,1)S(1)}, bf16[16,1,6,1792]{3,2,1,0:T(8,128)(2,1)S(1)}, u32[]{:S(2)}, u32[]{:S(2)}) collective-permute-start(bf16[16,1,6,1792]{3,2,1,0:T(8,128)(2,1)S(1)} %get-tuple-element.15), channel_id=1, source_target_pairs={{0,224},{16,240},{32,192},{48,208},{64,160},{80,176},{96,128},{112... | collective-permute-start | bytes 1032200 | tf_op jit(solution)/shard_map/ppermute | solution.py:20
  524.6 32.5 %collective-permute-start.16 = (bf16[16,1,6,1792]{3,2,1,0:T(8,128)(2,1)S(1)}, bf16[16,1,6,1792]{3,2,1,0:T(8,128)(2,1)S(1)}, u32[]{:S(2)}, u32[]{:S(2)}) collective-permute-start(bf16[16,1,6,1792]{3,2,1,0:T(8,128)(2,1)S(1)} %get-tuple-element.14), channel_id=1, source_target_pairs={{0,240},{16,224},{32,208},{48,192},{64,176},{80,160},{96,144},{112... | collective-permute-start | bytes 1032200 | tf_op jit(solution)/shard_map/ppermute | solution.py:20
  560.9 8.8 %copy-start.1 = (s32[64,8]{0,1:T(8,128)S(1)}, s32[64,8]{0,1:T(8,128)}, u32[]{:S(2)}) copy-start(s32[64,8]{0,1:T(8,128)} %param.12) | copy-start | bytes 6148
  560.9 127.1 %all-to-all-start.4 = ((bf16[16,16,6,1792]{3,1,2,0:T(8,128)(2,1)}), bf16[16,16,6,1792]{3,1,2,0:T(8,128)(2,1)}, u32[]{:S(2)}, u32[]{:S(2)}) async-start(bf16[16,16,6,1792]{3,1,2,0:T(8,128)(2,1)} %copy.150), calls=%async_computation.4 | async-start | bytes 11010048 | tf_op jit(solution)/shard_map/all_to_all | solution.py:135
